TPU v7x, 32 devices: a whole 2x2x4 slice. The times are simulated.
32 devices in a mesh: depth: 8 (over y, x, core), chan: 4 (over z).
Axes of the slice: x: 2, y: 2, z: 4, core: 2. Of those that a mesh axis runs over, the one named last changes fastest.
Arguments:
- grad_out: bfloat16 [128, 8, 32, 128], P('chan', 'depth'), may hold values from -6 to 6
- volume: bfloat16 [64, 16, 64, 256], P('chan', 'depth'), may hold values from -6 to 6
- weight: bfloat16 [27, 64, 128], replicated, may hold values from -0.15625 to 0.15625
Outputs:
- input_grad: bfloat16 [64, 16, 64, 256], P('chan', 'depth')
- weight_grad: float32 [27, 64, 128], P(None, 'chan', 'depth')
All inputs are finite; a program needn't handle non-finite values.
Results may differ from a plain program's by a relative error of at most 0.001.
Values may be sent and summed in bfloat16 or wider, within the bound.
No kernel may reach another device: no remote copies, remote signals or barrier semaphores. Data moves between devices by JAX's collectives and lax.ppermute only.
A program may use at most 192 MiB of HBM per device.

v0:
```python
import math

import jax
import jax.numpy as jnp
from jax import lax
from jax.sharding import PartitionSpec as P


def from_behind(shard, axis, by):
    count = lax.axis_size(axis)
    pairs = [(i, i + by) for i in range(count) if 0 <= i + by < count]
    return lax.ppermute(shard, axis, pairs)


def upsample(stacked, axis, extended):
    tap_zero, tap_one, tap_two = (stacked[0], stacked[1], stacked[2])
    coord_axis = axis - 1
    length = tap_zero.shape[coord_axis]
    if extended:
        outer = length - 1
        even_cells = lax.slice_in_dim(tap_one, 0, outer, axis=coord_axis)
        odd_cells = lax.slice_in_dim(tap_zero, 1, length, axis=coord_axis) + lax.slice_in_dim(
            tap_two, 0, outer, axis=coord_axis
        )
    else:
        outer = length
        shifted = lax.slice_in_dim(tap_zero, 1, length, axis=coord_axis)
        shifted = jnp.concatenate(
            [shifted, jnp.zeros_like(lax.slice_in_dim(tap_zero, 0, 1, axis=coord_axis))],
            axis=coord_axis,
        )
        even_cells = tap_one
        odd_cells = shifted + tap_two
    paired = jnp.stack([even_cells, odd_cells], axis=coord_axis + 1)
    new_shape = list(even_cells.shape)
    new_shape[coord_axis] = 2 * outer
    return paired.reshape(new_shape)


def phase_grads(weight_rows, grads_ext):
    local_in = weight_rows.shape[0] // 27
    channels_out, planes, rows, cols = grads_ext.shape
    taps_out = jnp.dot(
        weight_rows, grads_ext.reshape(channels_out, -1), preferred_element_type=jnp.float32
    )
    taps_out = taps_out.reshape(3, 3, 3, local_in, planes, rows, cols)
    along_w = upsample(jnp.moveaxis(taps_out, 2, 0), 6, False)
    along_h = upsample(jnp.moveaxis(along_w, 1, 0), 4, False)
    return upsample(along_h, 2, True)


def weight_terms(inputs, grads_ext):
    row_extra = 0
    weight_cube = lax.conv_general_dilated(
        inputs[None],
        grads_ext[:, None],
        (1, 1, 1),
        ((1, 2), (1, row_extra), (1, 0)),
        rhs_dilation=(2, 2, 2),
        dimension_numbers=("CNDHW", "OIDHW", "NCDHW"),
        preferred_element_type=jnp.float32,
    )
    return jnp.transpose(weight_cube, (2, 3, 4, 0, 1)).reshape(
        27, weight_cube.shape[0], weight_cube.shape[1]
    )


def shards(grad_out, volume, weight):
    plane_next = from_behind(grad_out, "depth", -1)
    grads_ext = jnp.concatenate([grad_out, plane_next], axis=1)
    channels_out = weight.shape[2]
    local_in = volume.shape[0]
    every_channel = lax.all_gather(grads_ext, "chan", axis=0, tiled=True)
    own_weight = lax.dynamic_slice_in_dim(weight, lax.axis_index("chan") * local_in, local_in, 1)
    input_part = phase_grads(own_weight.reshape(27 * local_in, channels_out), every_channel)
    weight_part = weight_terms(volume, every_channel)
    input_grad = input_part.astype(jnp.bfloat16)
    summed = lax.psum_scatter(weight_part, "depth", scatter_dimension=2, tiled=True)
    cell_count = grad_out.shape[1] * lax.axis_size("depth") * grad_out.shape[2] * grad_out.shape[3]
    return (input_grad, summed * (1.0 / math.sqrt(cell_count)))


def solution(mesh):
    in_specs = (P("chan", "depth", None, None), P("chan", "depth", None, None), P())
    out_specs = (P("chan", "depth", None, None), P(None, "chan", "depth"))
    return jax.shard_map(shards, mesh=mesh, in_specs=in_specs, out_specs=out_specs, check_vma=False)
```

profile of v0, /device:TPU:0, one launch (start us, length us, event | category | flops | bytes accessed | tf_op | source)
XLA Modules:
  0.0 334.6 jit_solution(5004048821338022070)
XLA Ops:
  7.2 0.0 copy-start
  7.2 0.0 all-gather.2.cloned.1.call-start
  7.2 1.4 collective-permute-start
  8.7 2.3 collective-permute-done
  11.0 1.8 pad_maximum_fusion.2
  12.8 0.0 all-gather.2.cloned.1.call-update
  12.8 0.0 reduce-scatter.2.cloned.1.call-start
  12.9 23.1 %copy.57 = bf16[1,16,2,64,256]{1,0,4,3,2:T(2,128)(2,1)} copy(bf16[1,16,2,64,256]{4,3,2,1,0:T(8,128)(2,1)} %bitcast.72) | data formatting | bytes 2097152 | tf_op jit(solution)/shard_map/broadcast_in_dim | solution.py:55
  36.0 0.0 copy-done
  36.0 29.3 %all-gather.2.cloned.1.call-done = bf16[128,2,32,128]{3,2,1,0:T(8,128)(2,1)} async-done(((bf16[32,2,32,128]{3,2,1,0:T(8,128)(2,1)}), bf16[128,2,32,128]{3,2,1,0:T(8,128)(2,1)}) %all-gather.2.cloned.1.call-update) | async-done | bytes 2097168 | tf_op jit(solution)/shard_map/all_gather | solution.py:73
  65.3 3.5 %copy.63 = bf16[128,2,32,128]{0,3,2,1:T(8,128)(2,1)S(1)} copy(bf16[128,2,32,128]{3,2,1,0:T(8,128)(2,1)} %all-gather.2.cloned.1.call-done) | data formatting | bytes 4194304 | tf_op jit(solution)/shard_map/reshape | solution.py:44
  68.8 2.0 convolution_bitcast_fusion
  70.8 3.2 slice_bitcast_fusion.5
  74.0 1.3 slice.63
  75.3 0.6 fusion.6
  75.9 7.0 %pad_maximum_fusion = f32[3,3,16,2,32,128,2]{5,2,4,3,1,0,6:T(8,128)} fusion(f32[3,3,16,2,32,128,1]{5,2,4,3,1,0,6:T(8,128)S(1)} %fusion.6, f32[3,3,16,2,32,128,1]{5,2,4,3,1,0,6:T(8,128)} %get-tuple-element.12), kind=kLoop, calls=%fused_computation.9 | loop fusion | flops 2359296 | bytes 18874368 | tf_op jit(solution)/shard_map/stack | solution.py:34
  82.9 29.5 %copy.64 = f32[3,3,16,2,32,128,2]{4,2,6,5,3,0,1:T(8,128)} copy(f32[3,3,16,2,32,128,2]{5,2,4,3,1,0,6:T(8,128)} %pad_maximum_fusion) | data formatting | bytes 18874368 | tf_op jit(solution)/shard_map/transpose | solution.py:48
  112.4 29.6 %copy.51 = f32[3,3,16,2,32,128,2]{4,2,6,5,3,1,0:T(8,128)} copy(f32[3,3,16,2,32,128,2]{5,2,4,3,1,0,6:T(8,128)} %pad_maximum_fusion) | data formatting | bytes 18874368 | tf_op jit(solution)/shard_map/stack | solution.py:34
  142.0 17.9 %slice_bitcast_fusion.2 = (f32[3,16,2,32,1,256]{3,1,5,2,0,4:T(8,128)}, f32[3,16,2,32,256]{3,1,4,2,0:T(8,128)}) fusion(f32[3,3,16,2,32,256]{4,2,5,3,1,0:T(8,128)} %bitcast.66), kind=kLoop, calls=%fused_computation.8 | loop fusion | bytes 12582912 | tf_op jit(solution)/shard_map/stack;squeeze | solution.py:34
  159.9 12.3 %slice.67 = f32[3,16,2,31,256]{3,1,4,2,0:T(8,128)} slice(f32[3,16,2,32,256]{3,1,4,2,0:T(8,128)} %get-tuple-element.9), slice={[0:3], [0:16], [0:2], [1:32], [0:256]} | slice | bytes 6094848 | tf_op jit(solution)/shard_map/slice | solution.py:27
  172.3 0.0 copy-start.2
  172.3 14.2 %fusion.1 = f32[3,16,2,32,1,256]{3,1,5,2,0,4:T(8,128)} fusion(f32[3,3,16,2,32,256]{4,2,5,3,0,1:T(8,128)} %bitcast.67, f32[3,16,2,31,256]{3,1,4,2,0:T(8,128)} %slice.67), kind=kLoop, calls=%fused_computation.6 | loop fusion | flops 786432 | bytes 9338880 | tf_op jit(solution)/shard_map/stack | solution.py:34
  186.5 2.1 copy-done.2
  188.6 3.9 %fusion.4 = bf16[1,16,2,32,2,256]{3,1,5,2,0,4:T(8,128)(2,1)} fusion(f32[3,16,2,32,1,256]{3,1,5,2,0,4:T(8,128)S(1)} %copy-done.2, f32[3,16,2,32,1,256]{3,1,5,2,0,4:T(8,128)} %fusion.1), kind=kLoop, calls=%fused_computation.12 | loop fusion | flops 524288 | bytes 7340032 | tf_op jit(solution)/shard_map/convert.6
  192.5 0.0 copy-start.3
  192.5 8.8 %fusion.2 = (f32[1,16,2,32,2,256]{3,1,5,2,0,4:T(8,128)}, f32[1,16,2,32,2,256]{3,1,5,2,0,4:T(8,128)}) fusion(f32[3,16,2,32,1,256]{3,1,5,2,0,4:T(8,128)S(1)} %copy-done.2, f32[3,16,2,32,1,256]{3,1,5,2,0,4:T(8,128)} %fusion.1), kind=kLoop, calls=%fused_computation.10 | loop fusion | flops 1048576 | bytes 10485760 | tf_op jit(solution)/shard_map/stack | solution.py:34
  201.3 0.0 copy-done.3
  201.3 5.0 %copy.58 = bf16[128,1,2,32,128]{0,1,4,3,2:T(2,128)(2,1)} copy(bf16[128,1,2,32,128]{4,3,2,0,1:T(8,128)(2,1)S(1)} %bitcast.68) | data formatting | bytes 4194304 | tf_op jit(solution)/shard_map/broadcast_in_dim | solution.py:56
  206.3 83.6 %fusion.10 = f32[3,3,3,16,128]{4,3,2,1,0:T(8,128)S(1)} fusion(bf16[1,16,2,64,256]{1,0,4,3,2:T(2,128)(2,1)} %copy.57, bf16[128,1,2,32,128]{0,1,4,3,2:T(2,128)(2,1)} %copy.58), kind=kOutput, calls=%fused_computation.29 | convolution fusion | flops 447098880 | bytes 3366912 | tf_op jit(solution)/shard_map/transpose | solution.py:63
  289.9 1.4 copy.59
  291.3 0.0 reduce-scatter.2.cloned.1.call-update
  291.3 6.9 %copy.54 = bf16[1,16,2,32,2,256]{5,1,4,3,2,0:T(8,128)(2,1)} copy(bf16[1,16,2,32,2,256]{3,1,5,2,0,4:T(8,128)(2,1)} %fusion.4) | data formatting | bytes 2097152 | tf_op jit(solution)/shard_map/slice | solution.py:16
  298.2 7.1 %copy.55 = f32[1,16,2,32,2,256]{5,1,4,3,2,0:T(8,128)S(1)} copy(f32[1,16,2,32,2,256]{3,1,5,2,0,4:T(8,128)} %get-tuple-element.10) | data formatting | bytes 4194304 | tf_op jit(solution)/shard_map/slice | solution.py:16
  305.3 0.0 copy-start.1
  305.3 8.0 %copy.56 = f32[1,16,2,32,2,256]{5,1,4,3,2,0:T(8,128)} copy(f32[1,16,2,32,2,256]{3,1,5,2,0,4:T(8,128)} %get-tuple-element.11) | data formatting | bytes 4194304 | tf_op jit(solution)/shard_map/slice | solution.py:16
  313.3 1.4 fusion.9
  314.7 1.1 slice_bitcast_fusion.6
  315.8 0.1 maximum_bitcast_fusion
  315.9 1.3 copy.60
  317.2 9.0 %reduce-scatter.2.cloned.1.call-done = f32[27,16,16]{0,2,1:T(8,128)} async-done(((f32[27,16,128]{0,2,1:T(8,128)}), f32[27,16,16]{0,2,1:T(8,128)}) %reduce-scatter.2.cloned.1.call-update) | async-done | bytes 27664 | tf_op jit(solution)/shard_map/reduce_scatter | solution.py:78
  326.2 1.6 broadcast_multiply_fusion
  327.8 0.0 copy-done.1
  (1 shorter events, 0.0 us)
Async XLA Ops:
  7.2 28.8 %copy-start = (bf16[27,64,128]{2,1,0:T(8,128)(2,1)S(1)}, bf16[27,64,128]{2,1,0:T(8,128)(2,1)}, u32[]{:S(2)}) copy-start(bf16[27,64,128]{2,1,0:T(8,128)(2,1)} %param.5) | copy-start | bytes 1327108
  7.2 58.1 %all-gather.2.cloned.1.call-start = ((), (), s32[]{:S(2)}) async-start(), calls=%async_computation.1 | async-start | bytes 2621440 | tf_op jit(solution)/shard_map/all_gather | solution.py:73
  7.2 3.8 %collective-permute-start = (bf16[32,1,32,128]{3,2,1,0:T(8,128)(2,1)}, bf16[32,1,32,128]{3,2,1,0:T(8,128)(2,1)S(1)}, u32[]{:S(2)}, u32[]{:S(2)}) collective-permute-start(bf16[32,1,32,128]{3,2,1,0:T(8,128)(2,1)} %param.3), channel_id=1, source_target_pairs={{4,0},{8,4},{12,8},{16,12},{20,16},{24,20},{28,24},{5,1},{9,5},{13... | collective-permute-start | bytes 786440 | tf_op jit(solution)/shard_map/ppermute | solution.py:12
  12.8 313.4 %reduce-scatter.2.cloned.1.call-start = ((), (), s32[]{:S(2)}) async-start(), calls=%async_computation.2 | async-start | bytes 1179648 | tf_op jit(solution)/shard_map/reduce_scatter | solution.py:78
  172.3 16.3 %copy-start.2 = (f32[3,16,2,32,1,256]{3,1,5,2,0,4:T(8,128)S(1)}, f32[3,16,2,32,1,256]{3,1,5,2,0,4:T(8,128)}, u32[]{:S(2)}) copy-start(f32[3,16,2,32,1,256]{3,1,5,2,0,4:T(8,128)} %get-tuple-element.8) | copy-start | bytes 9437188
  192.5 8.8 %copy-start.3 = (bf16[128,2,32,128]{3,2,1,0:T(8,128)(2,1)S(1)}, bf16[128,2,32,128]{3,2,1,0:T(8,128)(2,1)}, u32[]{:S(2)}) copy-start(bf16[128,2,32,128]{3,2,1,0:T(8,128)(2,1)} %all-gather.2.cloned.1.call-done) | copy-start | bytes 6291460
  305.3 22.5 %copy-start.1 = (bf16[27,64,128]{2,1,0:T(8,128)(2,1)S(1)}, bf16[27,64,128]{2,1,0:T(8,128)(2,1)}, u32[]{:S(2)}) copy-start(bf16[27,64,128]{2,1,0:T(8,128)(2,1)} %param.5) | copy-start | bytes 1327108
Sparse Core Ops, SparseCore 0:
  13.0 52.3 all-gather.1
  291.4 34.7 reduce-scatter.1
where the time goes:
time: 338 us; the launch traced here: 335 us
  local copies, waits for them, and re-layouts  153 us (45%)
  matrix products  85.6 us (25%)
  waiting for transfers between devices  40.7 us (12%)
  other arithmetic  39.4 us (12%)
  between operations  14.1 us (4%)
    transpose x1, matrix products, weight_terms(): jnp.transpose(weight_cube, (2, 3, 4, 0, 1))  83.6 us
    another operation x4, local copies, waits for them, and re-layouts, upsample(): paired = jnp.stack([even_cells, odd_cells], axis=coord_axis + 1)  51.8 us
    another operation x5, other arithmetic, upsample(): paired = jnp.stack([even_cells, odd_cells], axis=coord_axis + 1)  32 us
    transpose x1, local copies, waits for them, and re-layouts, phase_grads(): along_h = upsample(jnp.moveaxis(along_w, 1, 0), 4, False)  29.5 us
    all_gather x1, waiting for transfers between devices, shards(): every_channel = lax.all_gather(grads_ext, 'chan', axis=0, tiled=True)  29.3 us
    broadcast_in_dim x1, local copies, waits for them, and re-layouts, weight_terms(): inputs[None]  23.1 us
    slice x3, local copies, waits for them, and re-layouts, upsample(): tap_zero, tap_one, tap_two = (stacked[0], stacked[1], stacked[2])  22 us
    slice x2, local copies, waits for them, and re-layouts, upsample(): shifted = lax.slice_in_dim(tap_zero, 1, length, axis=coord_axis)  13.6 us
  transfers between devices with their start and end apart: 3, of which 3 were waited for; matrix products, arithmetic and copies ran while one was open for 15% of the time, Pallas kernels for 0%

commit v1 on v0

--- a/solution.py
+++ b/solution.py
@@ -3,7 +3,157 @@
 import jax
 import jax.numpy as jnp
 from jax import lax
+from jax.experimental import pallas as pl
+from jax.experimental.pallas import tpu as pltpu
 from jax.sharding import PartitionSpec as P
+
+F32 = jnp.float32
+BF16 = jnp.bfloat16
+VMEM = pl.BlockSpec(memory_space=pltpu.VMEM)
+SMEM = pl.BlockSpec(memory_space=pltpu.SMEM)
+LIMIT = 48 * 1024 * 1024
+
+
+def ring_order(count):
+    return [0] + list(range(1, count, 2)) + list(range(2, count, 2))[::-1]
+
+
+def matmul(left, right):
+    return jnp.dot(left, right, preferred_element_type=F32)
+
+
+def one_hot(rows, cols, source):
+    row = lax.broadcasted_iota(jnp.int32, (rows, cols), 0)
+    col = lax.broadcasted_iota(jnp.int32, (rows, cols), 1)
+    return jnp.where(source(row, col), 1.0, 0.0).astype(BF16)
+
+
+def swap_rows(major, minor):
+    bits = minor.bit_length() - 1
+    return one_hot(
+        major * minor,
+        major * minor,
+        lambda row, col: col == (row & (minor - 1)) * major + (row >> bits),
+    )
+
+
+def volume_kernel(v_ref, m_ref):
+    chans, _, rows, cols = v_ref.shape
+    half = cols // 2
+    group = 256 // chans
+    swap = swap_rows(group, chans)
+    split = one_hot(cols, 3 * half, lambda row, col: row == 2 * (col & (half - 1)) + col // half - 1)
+    for plane in range(2):
+        base = plane * 9 * chans
+        for start in range(0, rows, group):
+            block = v_ref[:, plane, start : start + group, :].reshape(chans * group, cols)
+            by_row = matmul(swap, block).astype(BF16)
+            views = matmul(by_row, split).astype(BF16)
+            for at in range(group):
+                row = start + at
+                for e in range(3):
+                    piece = views[at * chans : (at + 1) * chans, e * half : (e + 1) * half]
+                    if row % 2 == 0:
+                        places = [(1, row // 2)]
+                    else:
+                        places = [(2, row // 2), (0, row // 2 + 1)]
+                    for b, r in places:
+                        if r < rows // 2:
+                            lo = base + (3 * b + e) * chans
+                            m_ref[lo : lo + chans, r * half : (r + 1) * half] = piece
+        m_ref[base : base + 3 * chans, :half] = jnp.zeros((3 * chans, half), BF16)
+
+
+def grads_kernel(at_ref, *refs):
+    parts = len(refs) // 2 - 1
+    m_ref, stack_ref, wt_ref = refs[2 * parts], refs[2 * parts + 1], refs[2 * parts + 2]
+    _, _, rows, cols = refs[0].shape
+    channels = stack_ref.shape[0] // 4
+    swap = swap_rows(16, 16)
+    ahead = one_hot(cols, cols, lambda row, col: row == col + 1)
+    for index in range(2 * parts):
+        ref = refs[index]
+        own = index < parts
+        plain_base = 2 * channels if own else channels
+        ahead_base = 3 * channels if own else 0
+        for o in range(0, ref.shape[0], 16):
+            place = pl.multiple_of(at_ref[index % parts] + o, 16)
+            for h in range(0, rows, 16):
+                block = ref[o : o + 16, 0, h : h + 16, :].reshape(256, cols)
+                by_row = matmul(swap, block).astype(BF16)
+                moved = matmul(by_row, ahead).astype(BF16)
+                for k in range(16):
+                    lanes = slice((h + k) * cols, (h + k + 1) * cols)
+                    stack_ref[pl.ds(plain_base + place, 16), lanes] = by_row[16 * k : 16 * k + 16]
+                    stack_ref[pl.ds(ahead_base + place, 16), lanes] = moved[16 * k : 16 * k + 16]
+    third = m_ref.shape[0] // 2
+    contract = (((1,), (1,)), ((), ()))
+    wt_ref[:, :third] = lax.dot_general(
+        stack_ref[channels : 2 * channels, :], m_ref[third:, :], contract, preferred_element_type=F32
+    )
+    wt_ref[:, third:] = lax.dot_general(
+        stack_ref[2 * channels : 3 * channels, :], m_ref[...], contract, preferred_element_type=F32
+    )
+
+
+def input_kernel(w_ref, stack_ref, out_ref, lhs_ref, taps_ref):
+    chans, _, rows, cols = out_ref.shape
+    channels = w_ref.shape[2]
+    half = cols // 2
+    zero = jnp.zeros((chans, channels), BF16)
+    tap = lambda a, b, e: w_ref[9 * a + 3 * b + e]
+    for b in range(3):
+        for k, line in enumerate(
+            (
+                (zero, zero, tap(1, b, 1), zero),
+                (zero, zero, tap(1, b, 2), tap(1, b, 0)),
+                (zero, tap(0, b, 1), tap(2, b, 1), zero),
+                (tap(0, b, 0), tap(0, b, 2), tap(2, b, 2), tap(2, b, 0)),
+            )
+        ):
+            lo = (3 * k + b) * chans
+            for q, block in enumerate(line):
+                lhs_ref[lo : lo + chans, q * channels : (q + 1) * channels] = block
+    grid_cells = stack_ref.shape[1]
+    taps_ref[:, :grid_cells] = matmul(lhs_ref[...], stack_ref[...])
+    taps_ref[:, grid_cells:] = jnp.zeros((taps_ref.shape[0], half), F32)
+    group = 256 // chans
+    swap = swap_rows(chans, group)
+    weave = one_hot(cols, cols, lambda row, col: col == 2 * (row & (half - 1)) + row // half)
+
+    def cells(plane, side, b, r):
+        lo = ((plane * 2 + side) * 3 + b) * chans
+        return taps_ref[lo : lo + chans, r * half : (r + 1) * half]
+
+    for plane in range(2):
+        for start in range(0, rows, group):
+            pieces = []
+            for row in range(start, start + group):
+                r = row // 2
+                if row % 2 == 0:
+                    both = [cells(plane, side, 1, r) for side in range(2)]
+                else:
+                    both = [cells(plane, side, 0, r + 1) + cells(plane, side, 2, r) for side in range(2)]
+                pieces.append(jnp.concatenate(both, axis=1).astype(BF16))
+            block = jnp.concatenate(pieces, axis=0)
+            woven = matmul(block, weave).astype(BF16)
+            placed = matmul(swap, woven).astype(BF16)
+            out_ref[:, plane, start : start + group, :] = placed.reshape(chans, group, cols)
+
+
+def total_kernel(scale, r_ref, out_ref):
+    chans, outs, taps = out_ref.shape
+    total = r_ref[0]
+    for source in range(1, r_ref.shape[0]):
+        total = total + r_ref[source]
+    total = total * scale
+    bits = chans.bit_length() - 1
+    order = one_hot(
+        taps * chans, 32 * chans, lambda row, col: row == (col & 31) * chans + (col >> 5)
+    ).astype(F32)
+    by_chan = jnp.dot(total, order, precision=lax.Precision.HIGHEST, preferred_element_type=F32)
+    for c in range(chans):
+        out_ref[c] = by_chan[:, 32 * c : 32 * c + taps]
 
 
 def from_behind(shard, axis, by):
@@ -65,7 +215,7 @@
     )
 
 
-def shards(grad_out, volume, weight):
+def plain_shards(grad_out, volume, weight):
     plane_next = from_behind(grad_out, "depth", -1)
     grads_ext = jnp.concatenate([grad_out, plane_next], axis=1)
     channels_out = weight.shape[2]
@@ -80,7 +230,96 @@
     return (input_grad, summed * (1.0 / math.sqrt(cell_count)))
 
 
+def call(kernel, out_shape, *args, specs=None, scratch=(), cost=None):
+    flops, moved = cost
+    return pl.pallas_call(
+        kernel,
+        out_shape=out_shape,
+        in_specs=specs or [VMEM] * len(args),
+        out_specs=jax.tree.map(lambda _: VMEM, out_shape),
+        scratch_shapes=scratch,
+        compiler_params=pltpu.CompilerParams(vmem_limit_bytes=LIMIT),
+        cost_estimate=pl.CostEstimate(flops=flops, bytes_accessed=moved, transcendentals=0),
+    )(*args)
+
+
+def shards(grad_out, volume, weight):
+    count = lax.axis_size("chan")
+    depth = lax.axis_size("depth")
+    own_outs, _, rows, cols = grad_out.shape
+    chans = volume.shape[0]
+    channels = weight.shape[2]
+    cells = rows * cols
+    order = ring_order(count)
+    ahead = [(order[i], order[(i + 1) % count]) for i in range(count)]
+    back = [(b, a) for a, b in ahead]
+    nearer = [(i, i - 1) for i in range(1, depth)]
+    mine = lax.axis_index("chan")
+    seats = [order.index(i) for i in range(count)]
+    holders = lambda shift, extra=0: [order[(seat + shift) % count] * own_outs + extra for seat in seats]
+
+    parts = [grad_out]
+    places = [holders(0)]
+    up = down = grad_out
+    for step in range(1, (count - 1) // 2 + 1):
+        up = lax.ppermute(up, "chan", ahead)
+        down = lax.ppermute(down, "chan", back)
+        parts += [up, down]
+        places += [holders(-step), holders(step)]
+    if count % 2 == 0:
+        middle = own_outs // 2
+        parts += [lax.ppermute(up[:middle], "chan", ahead), lax.ppermute(down[middle:], "chan", back)]
+        places += [holders(count // 2), holders(count // 2, middle)]
+    nexts = [lax.ppermute(part, "depth", nearer) for part in parts]
+
+    unfolded = call(
+        volume_kernel,
+        jax.ShapeDtypeStruct((18 * chans, cells), BF16),
+        volume,
+        cost=(2 * 2 * 64 * 256 * 640 * chans, 4 << 20),
+    )
+    own_weight = lax.dynamic_slice_in_dim(weight, mine * chans, chans, 1)
+    stack, partial = call(
+        grads_kernel,
+        (
+            jax.ShapeDtypeStruct((4 * channels, cells), BF16),
+            jax.ShapeDtypeStruct((channels, 27 * chans), F32),
+        ),
+        lax.dynamic_index_in_dim(jnp.asarray(places, jnp.int32).T, mine, 0, keepdims=False),
+        *parts,
+        *nexts,
+        unfolded,
+        specs=[SMEM] + [VMEM] * (2 * len(parts) + 1),
+        cost=(2 * 27 * chans * channels * cells * 4, 8 << 20),
+    )
+    terms = lax.all_to_all(partial, "depth", split_axis=0, concat_axis=0, tiled=True)
+    input_grad = call(
+        input_kernel,
+        jax.ShapeDtypeStruct(volume.shape, BF16),
+        own_weight,
+        stack,
+        scratch=(
+            pltpu.VMEM((12 * chans, 4 * channels), BF16),
+            pltpu.VMEM((12 * chans, cells + cols), F32),
+        ),
+        cost=(2 * 12 * chans * 4 * channels * cells, 8 << 20),
+    )
+    scale = 1.0 / math.sqrt(depth * cells)
+    outs = channels // depth
+    weight_grad = call(
+        lambda r, o: total_kernel(scale, r, o),
+        jax.ShapeDtypeStruct((chans, outs, 27), F32),
+        terms.reshape(depth, outs, 27 * chans),
+        cost=(1 << 20, 1 << 20),
+    )
+    return input_grad, jnp.transpose(weight_grad, (2, 0, 1))
+
+
 def solution(mesh):
     in_specs = (P("chan", "depth", None, None), P("chan", "depth", None, None), P())
     out_specs = (P("chan", "depth", None, None), P(None, "chan", "depth"))
-    return jax.shard_map(shards, mesh=mesh, in_specs=in_specs, out_specs=out_specs, check_vma=False)
+    def either(grad_out, volume, weight):
+        fits = grad_out.shape[0] % 32 == 0 and volume.shape[0] == 16 and grad_out.shape[1] == 1
+        return (shards if fits else plain_shards)(grad_out, volume, weight)
+
+    return jax.shard_map(either, mesh=mesh, in_specs=in_specs, out_specs=out_specs, check_vma=False)

time: 338 us -> 58.8 us (0.17)
  local copies, waits for them, and re-layouts: 153 us -> 5.09 us
  matrix products: 85.6 us -> 0 us
  other arithmetic: 39.4 us -> 0 us
  waiting for transfers between devices: 40.7 us -> 9.65 us
  starting transfers between devices: 1.5 us -> 27.7 us
  Pallas kernels: 0 us -> 15.1 us
  between operations: 14.1 us -> 0.74 us
    transpose x1 -> x0, matrix products: 83.6 us -> none  [weight_terms(): jnp.transpose(weight_cube, (2, 3, 4, 0, 1))]
    another operation x4 -> x0, local copies, waits for them, and re-layouts: 51.8 us -> none  [upsample(): paired = jnp.stack([even_cells, odd_cells], axis=coord_axis + 1)]
    another operation x6 -> x0, other arithmetic: 35.9 us -> none  [the longest x5 32 us: upsample(): paired = jnp.stack([even_cells, odd_cells], axis=coord_axis + 1)]
    slice x5 -> x2, local copies, waits for them, and re-layouts: 35.6 us -> 0.02 us  [the longest x1 0.01 us: shards(): up[:middle]]
    transpose x1 -> x0, local copies, waits for them, and re-layouts: 29.5 us -> none  [phase_grads(): along_h = upsample(jnp.moveaxis(along_w, 1, 0), 4, False)]
    all_gather x1 -> x0, waiting for transfers between devices: 29.3 us -> none  [shards(): every_channel = lax.all_gather(grads_ext, 'chan', axis=0, tiled=True)]
    broadcast_in_dim x2 -> x0, local copies, waits for them, and re-layouts: 28.1 us -> none  [the longest x1 23.1 us: weight_terms(): inputs[None]]
    ppermute x1 -> x9, starting transfers between devices: 1.42 us -> 19 us  [the longest x1 7.41 us: shards(): lax.ppermute(up[:middle], 'chan', ahead)]
  transfers between devices with their start and end apart: 3 -> 10, of which waited for: 3 -> 4; matrix products, arithmetic and copies ran while one was open for 15% -> 1% of each run, Pallas kernels for 0% -> 8%
where the time goes in v1:
time: 58.8 us; the launch traced here: 58.3 us
  starting transfers between devices  27.7 us (47%)
  Pallas kernels  15.1 us (26%)
  waiting for transfers between devices  9.65 us (16%)
  local copies, waits for them, and re-layouts  5.09 us (9%)
  between operations  0.74 us (1%)
    pallas_call x4, Pallas kernels, call(): pl.pallas_call(kernel, out_shape=out_shape, in_specs=specs or [VMEM] * le...  15.1 us
    all_to_all x1, starting transfers between devices, shards(): lax.all_to_all(partial, 'depth', split_axis=0, concat_axis=0, tiled=True)  8.76 us
    ppermute x1, starting transfers between devices, shards(): lax.ppermute(up[:middle], 'chan', ahead)  7.41 us
    ppermute x1, waiting for transfers between devices, shards(): up = lax.ppermute(up, 'chan', ahead)  6.55 us
    ppermute x5, starting transfers between devices, shards(): nexts = [lax.ppermute(part, 'depth', nearer) for part in parts]  6.44 us
    unnamed x8, local copies, waits for them, and re-layouts  4.36 us
    ppermute x1, starting transfers between devices, shards(): up = lax.ppermute(up, 'chan', ahead)  3.08 us
    all_to_all x1, waiting for transfers between devices, shards(): lax.all_to_all(partial, 'depth', split_axis=0, concat_axis=0, tiled=True)  2.02 us
  transfers between devices with their start and end apart: 10, of which 4 were waited for; matrix products, arithmetic and copies ran while one was open for 1% of the time, Pallas kernels for 8%

profile of v1, /device:TPU:0, one launch (start us, length us, event | category | flops | bytes accessed | tf_op | source)
XLA Modules:
  0.0 58.3 jit_solution(3003535038410166597)
XLA Ops:
  0.6 0.0 copy-start
  0.6 3.1 %collective-permute-start = (bf16[32,1,32,128]{3,2,1,0:T(8,128)(2,1)}, bf16[32,1,32,128]{3,2,1,0:T(8,128)(2,1)S(1)}, u32[]{:S(2)}, u32[]{:S(2)}) collective-permute-start(bf16[32,1,32,128]{3,2,1,0:T(8,128)(2,1)} %refs_0_.1), channel_id=1, source_target_pairs={{0,1},{1,3},{3,2},{2,0},{4,5},{5,7},{7,6},{6,4},{8,9},{9,11},{11,1... | collective-permute-start | bytes 786440 | tf_op jit(solution)/shard_map/ppermute | solution.py:265
  3.7 1.1 %collective-permute-start.1 = (bf16[32,1,32,128]{3,2,1,0:T(8,128)(2,1)}, bf16[32,1,32,128]{3,2,1,0:T(8,128)(2,1)S(1)}, u32[]{:S(2)}, u32[]{:S(2)}) collective-permute-start(bf16[32,1,32,128]{3,2,1,0:T(8,128)(2,1)} %refs_0_.1), channel_id=1, source_target_pairs={{1,0},{3,1},{2,3},{0,2},{5,4},{7,5},{6,7},{4,6},{9,8},{11,9},{10,1... | collective-permute-start | bytes 786440 | tf_op jit(solution)/shard_map/ppermute | solution.py:266
  4.8 6.6 %collective-permute-done.refs_1_ = bf16[32,1,32,128]{3,2,1,0:T(8,128)(2,1)S(1)} collective-permute-done((bf16[32,1,32,128]{3,2,1,0:T(8,128)(2,1)}, bf16[32,1,32,128]{3,2,1,0:T(8,128)(2,1)S(1)}, u32[]{:S(2)}, u32[]{:S(2)}) %collective-permute-start) | collective-permute-done | bytes 262176 | tf_op jit(solution)/shard_map/ppermute | solution.py:265
  11.4 7.4 %collective-permute-start.2 = (bf16[16,1,32,128]{3,2,1,0:T(8,128)(2,1)S(1)}, bf16[16,1,32,128]{3,2,1,0:T(8,128)(2,1)S(1)}, u32[]{:S(2)}, u32[]{:S(2)}) collective-permute-start(bf16[16,1,32,128]{3,2,1,0:T(8,128)(2,1)S(1)} %slice.8), channel_id=1, source_target_pairs={{0,1},{1,3},{3,2},{2,0},{4,5},{5,7},{7,6},{6,4},{8,9},{9,11},{11,1... | collective-permute-start | bytes 393224 | tf_op jit(solution)/shard_map/ppermute | solution.py:271
  18.8 0.0 collective-permute-done.1.refs_2_
  18.8 1.0 %collective-permute-start.3 = (bf16[16,1,32,128]{3,2,1,0:T(8,128)(2,1)S(1)}, bf16[16,1,32,128]{3,2,1,0:T(8,128)(2,1)}, u32[]{:S(2)}, u32[]{:S(2)}) collective-permute-start(bf16[16,1,32,128]{3,2,1,0:T(8,128)(2,1)S(1)} %slice.9), channel_id=1, source_target_pairs={{1,0},{3,1},{2,3},{0,2},{5,4},{7,5},{6,7},{4,6},{9,8},{11,9},{10,1... | collective-permute-start | bytes 393224 | tf_op jit(solution)/shard_map/ppermute | solution.py:271
  19.8 1.3 %collective-permute-start.4 = (bf16[32,1,32,128]{3,2,1,0:T(8,128)(2,1)}, bf16[32,1,32,128]{3,2,1,0:T(8,128)(2,1)}, u32[]{:S(2)}, u32[]{:S(2)}) collective-permute-start(bf16[32,1,32,128]{3,2,1,0:T(8,128)(2,1)} %refs_0_.1), channel_id=1, source_target_pairs={{4,0},{8,4},{12,8},{16,12},{20,16},{24,20},{28,24},{5,1},{9,5},{13... | collective-permute-start | bytes 786440 | tf_op jit(solution)/shard_map/ppermute | solution.py:273
  21.0 1.3 %collective-permute-start.5 = (bf16[32,1,32,128]{3,2,1,0:T(8,128)(2,1)S(1)}, bf16[32,1,32,128]{3,2,1,0:T(8,128)(2,1)}, u32[]{:S(2)}, u32[]{:S(2)}) collective-permute-start(bf16[32,1,32,128]{3,2,1,0:T(8,128)(2,1)S(1)} %collective-permute-done.refs_1_), channel_id=1, source_target_pairs={{4,0},{8,4},{12,8},{16,12},{20,16},{24,20},{28,24},{5,1},{9,5},{13... | collective-permute-start | bytes 786440 | tf_op jit(solution)/shard_map/ppermute | solution.py:273
  22.3 1.3 %collective-permute-start.6 = (bf16[32,1,32,128]{3,2,1,0:T(8,128)(2,1)S(1)}, bf16[32,1,32,128]{3,2,1,0:T(8,128)(2,1)}, u32[]{:S(2)}, u32[]{:S(2)}) collective-permute-start(bf16[32,1,32,128]{3,2,1,0:T(8,128)(2,1)S(1)} %collective-permute-done.1.refs_2_), channel_id=1, source_target_pairs={{4,0},{8,4},{12,8},{16,12},{20,16},{24,20},{28,24},{5,1},{9,5},{13... | collective-permute-start | bytes 786440 | tf_op jit(solution)/shard_map/ppermute | solution.py:273
  23.6 0.0 collective-permute-done.2.refs_3_
  23.7 1.3 %collective-permute-start.7 = (bf16[16,1,32,128]{3,2,1,0:T(8,128)(2,1)S(1)}, bf16[16,1,32,128]{3,2,1,0:T(8,128)(2,1)}, u32[]{:S(2)}, u32[]{:S(2)}) collective-permute-start(bf16[16,1,32,128]{3,2,1,0:T(8,128)(2,1)S(1)} %collective-permute-done.2.refs_3_), channel_id=1, source_target_pairs={{4,0},{8,4},{12,8},{16,12},{20,16},{24,20},{28,24},{5,1},{9,5},{13... | collective-permute-start | bytes 393224 | tf_op jit(solution)/shard_map/ppermute | solution.py:273
  25.0 0.3 collective-permute-done.3.refs_4_
  25.3 1.3 %collective-permute-start.8 = (bf16[16,1,32,128]{3,2,1,0:T(8,128)(2,1)}, bf16[16,1,32,128]{3,2,1,0:T(8,128)(2,1)}, u32[]{:S(2)}, u32[]{:S(2)}) collective-permute-start(bf16[16,1,32,128]{3,2,1,0:T(8,128)(2,1)} %collective-permute-done.3.refs_4_), channel_id=1, source_target_pairs={{4,0},{8,4},{12,8},{16,12},{20,16},{24,20},{28,24},{5,1},{9,5},{13... | collective-permute-start | bytes 393224 | tf_op jit(solution)/shard_map/ppermute | solution.py:273
  26.6 0.0 copy-start.2
  26.6 1.2 %copy-done.2 = bf16[16,2,64,256]{3,2,1,0:T(8,128)(2,1)S(1)} copy-done((bf16[16,2,64,256]{3,2,1,0:T(8,128)(2,1)S(1)}, bf16[16,2,64,256]{3,2,1,0:T(8,128)(2,1)}, u32[]{:S(2)}) %copy-start.2) | copy-done | bytes 1048600
  27.8 1.8 %shard_map.59.refs_10_ = bf16[288,4096]{1,0:T(8,128)(2,1)S(1)} custom-call(bf16[16,2,64,256]{3,2,1,0:T(8,128)(2,1)S(1)} %copy-done.2), custom_call_target="tpu_custom_call" | custom-call | flops 671088640 | bytes 4194304 | tf_op jit(solution)/shard_map/pallas_call | solution.py:235
  29.6 0.7 %dynamic-slice_bitcast_fusion.at_ref = s32[5]{0:T(128)S(1)} fusion(s32[5,4]{0,1:T(4,128)} %constant.17.clone, s32[]{:T(128)S(6)} %select_n.8), kind=kLoop, calls=%fused_computation | loop fusion | bytes 44 | tf_op jit(solution)/shard_map/jit(dynamic_index_in_dim)/squeeze | solution.py:288
  30.3 0.0 collective-permute-done.4.refs_5_
  30.3 0.0 collective-permute-done.7.refs_8_
  30.3 0.7 %collective-permute-done.8.refs_9_ = bf16[16,1,32,128]{3,2,1,0:T(8,128)(2,1)} collective-permute-done((bf16[16,1,32,128]{3,2,1,0:T(8,128)(2,1)}, bf16[16,1,32,128]{3,2,1,0:T(8,128)(2,1)}, u32[]{:S(2)}, u32[]{:S(2)}) %collective-permute-start.8) | collective-permute-done | bytes 131104 | tf_op jit(solution)/shard_map/ppermute | solution.py:273
  31.1 0.0 collective-permute-done.5.refs_6_
  31.1 0.0 collective-permute-done.6.refs_7_
  31.1 0.0 copy-start.3
  31.1 0.9 %copy-done.3 = bf16[32,1,32,128]{3,2,1,0:T(8,128)(2,1)S(1)} copy-done((bf16[32,1,32,128]{3,2,1,0:T(8,128)(2,1)S(1)}, bf16[32,1,32,128]{3,2,1,0:T(8,128)(2,1)}, u32[]{:S(2)}) %copy-start.3) | copy-done | bytes 262168
  32.0 9.2 %shard_map.60 = (bf16[512,4096]{1,0:T(8,128)(2,1)}, f32[128,432]{1,0:T(8,128)}) custom-call(s32[5]{0:T(128)S(1)} %dynamic-slice_bitcast_fusion.at_ref, bf16[32,1,32,128]{3,2,1,0:T(8,128)(2,1)S(1)} %copy-done.3, bf16[32,1,32,128]{3,2,1,0:T(8,128)(2,1)S(1)} %collective-permute-done.refs_1_, bf16[32,1,32,128]{3,2,1,0:T(8,128)(2,1)S(1)} %collective-permute-done.1.refs_2_, ...), custom_call_target="tpu_custom_call" | custom-call | flops 1811939328 | bytes 8388608 | tf_op jit(solution)/shard_map/pallas_call | solution.py:235
  41.3 8.8 %all-to-all-start = ((f32[8,16,432]{2,1,0:T(8,128)}), f32[8,16,432]{2,1,0:T(8,128)S(1)}, u32[]{:S(2)}, u32[]{:S(2)}) async-start(f32[8,16,432]{2,1,0:T(8,128)} %bitcast.1), calls=%async_computation | async-start | bytes 524288 | tf_op jit(solution)/shard_map/all_to_all | solution.py:295
  50.0 0.0 copy-done
  50.1 0.0 copy-start.1
  50.1 2.2 %copy-done.1 = bf16[512,4096]{1,0:T(8,128)(2,1)S(1)} copy-done((bf16[512,4096]{1,0:T(8,128)(2,1)S(1)}, bf16[512,4096]{1,0:T(8,128)(2,1)}, u32[]{:S(2)}) %copy-start.1) | copy-done | bytes 4194328
  52.3 2.7 %shard_map.61 = bf16[16,2,64,256]{3,2,1,0:T(8,128)(2,1)} custom-call(bf16[27,16,128]{2,1,0:T(8,128)(2,1)S(1)} %constant_dynamic-slice_fusion.w_ref, bf16[512,4096]{1,0:T(8,128)(2,1)S(1)} %copy-done.1), custom_call_target="tpu_custom_call" | custom-call | flops 805306368 | bytes 8388608 | tf_op jit(solution)/shard_map/pallas_call | solution.py:235
  55.0 2.0 %all-to-all-done.r = f32[8,16,432]{2,1,0:T(8,128)S(1)} async-done(((f32[8,16,432]{2,1,0:T(8,128)}), f32[8,16,432]{2,1,0:T(8,128)S(1)}, u32[]{:S(2)}, u32[]{:S(2)}) %all-to-all-start) | async-done | bytes 221216 | tf_op jit(solution)/shard_map/all_to_all | solution.py:295
  57.0 1.3 %shard_map.62 = f32[16,16,27]{2,1,0:T(8,128)} custom-call(f32[8,16,432]{2,1,0:T(8,128)S(1)} %all-to-all-done.r), custom_call_target="tpu_custom_call" | custom-call | flops 1048576 | bytes 1048576 | tf_op jit(solution)/shard_map/pallas_call | solution.py:235
  (3 shorter events, 0.0 us)
Async XLA Ops:
  0.6 49.4 %copy-start = (bf16[27,64,128]{2,1,0:T(8,128)(2,1)S(1)}, bf16[27,64,128]{2,1,0:T(8,128)(2,1)}, u32[]{:S(2)}) copy-start(bf16[27,64,128]{2,1,0:T(8,128)(2,1)} %param.6) | copy-start | bytes 1327108
  0.6 10.7 %collective-permute-start = (bf16[32,1,32,128]{3,2,1,0:T(8,128)(2,1)}, bf16[32,1,32,128]{3,2,1,0:T(8,128)(2,1)S(1)}, u32[]{:S(2)}, u32[]{:S(2)}) collective-permute-start(bf16[32,1,32,128]{3,2,1,0:T(8,128)(2,1)} %refs_0_.1), channel_id=1, source_target_pairs={{0,1},{1,3},{3,2},{2,0},{4,5},{5,7},{7,6},{6,4},{8,9},{9,11},{11,1... | collective-permute-start | bytes 786440 | tf_op jit(solution)/shard_map/ppermute | solution.py:265
  3.7 15.1 %collective-permute-start.1 = (bf16[32,1,32,128]{3,2,1,0:T(8,128)(2,1)}, bf16[32,1,32,128]{3,2,1,0:T(8,128)(2,1)S(1)}, u32[]{:S(2)}, u32[]{:S(2)}) collective-permute-start(bf16[32,1,32,128]{3,2,1,0:T(8,128)(2,1)} %refs_0_.1), channel_id=1, source_target_pairs={{1,0},{3,1},{2,3},{0,2},{5,4},{7,5},{6,7},{4,6},{9,8},{11,9},{10,1... | collective-permute-start | bytes 786440 | tf_op jit(solution)/shard_map/ppermute | solution.py:266
  11.4 12.3 %collective-permute-start.2 = (bf16[16,1,32,128]{3,2,1,0:T(8,128)(2,1)S(1)}, bf16[16,1,32,128]{3,2,1,0:T(8,128)(2,1)S(1)}, u32[]{:S(2)}, u32[]{:S(2)}) collective-permute-start(bf16[16,1,32,128]{3,2,1,0:T(8,128)(2,1)S(1)} %slice.8), channel_id=1, source_target_pairs={{0,1},{1,3},{3,2},{2,0},{4,5},{5,7},{7,6},{6,4},{8,9},{9,11},{11,1... | collective-permute-start | bytes 393224 | tf_op jit(solution)/shard_map/ppermute | solution.py:271
  18.8 6.5 %collective-permute-start.3 = (bf16[16,1,32,128]{3,2,1,0:T(8,128)(2,1)S(1)}, bf16[16,1,32,128]{3,2,1,0:T(8,128)(2,1)}, u32[]{:S(2)}, u32[]{:S(2)}) collective-permute-start(bf16[16,1,32,128]{3,2,1,0:T(8,128)(2,1)S(1)} %slice.9), channel_id=1, source_target_pairs={{1,0},{3,1},{2,3},{0,2},{5,4},{7,5},{6,7},{4,6},{9,8},{11,9},{10,1... | collective-permute-start | bytes 393224 | tf_op jit(solution)/shard_map/ppermute | solution.py:271
  19.8 10.6 %collective-permute-start.4 = (bf16[32,1,32,128]{3,2,1,0:T(8,128)(2,1)}, bf16[32,1,32,128]{3,2,1,0:T(8,128)(2,1)}, u32[]{:S(2)}, u32[]{:S(2)}) collective-permute-start(bf16[32,1,32,128]{3,2,1,0:T(8,128)(2,1)} %refs_0_.1), channel_id=1, source_target_pairs={{4,0},{8,4},{12,8},{16,12},{20,16},{24,20},{28,24},{5,1},{9,5},{13... | collective-permute-start | bytes 786440 | tf_op jit(solution)/shard_map/ppermute | solution.py:273
  21.0 10.0 %collective-permute-start.5 = (bf16[32,1,32,128]{3,2,1,0:T(8,128)(2,1)S(1)}, bf16[32,1,32,128]{3,2,1,0:T(8,128)(2,1)}, u32[]{:S(2)}, u32[]{:S(2)}) collective-permute-start(bf16[32,1,32,128]{3,2,1,0:T(8,128)(2,1)S(1)} %collective-permute-done.refs_1_), channel_id=1, source_target_pairs={{4,0},{8,4},{12,8},{16,12},{20,16},{24,20},{28,24},{5,1},{9,5},{13... | collective-permute-start | bytes 786440 | tf_op jit(solution)/shard_map/ppermute | solution.py:273
  22.3 8.7 %collective-permute-start.6 = (bf16[32,1,32,128]{3,2,1,0:T(8,128)(2,1)S(1)}, bf16[32,1,32,128]{3,2,1,0:T(8,128)(2,1)}, u32[]{:S(2)}, u32[]{:S(2)}) collective-permute-start(bf16[32,1,32,128]{3,2,1,0:T(8,128)(2,1)S(1)} %collective-permute-done.1.refs_2_), channel_id=1, source_target_pairs={{4,0},{8,4},{12,8},{16,12},{20,16},{24,20},{28,24},{5,1},{9,5},{13... | collective-permute-start | bytes 786440 | tf_op jit(solution)/shard_map/ppermute | solution.py:273
  23.7 6.7 %collective-permute-start.7 = (bf16[16,1,32,128]{3,2,1,0:T(8,128)(2,1)S(1)}, bf16[16,1,32,128]{3,2,1,0:T(8,128)(2,1)}, u32[]{:S(2)}, u32[]{:S(2)}) collective-permute-start(bf16[16,1,32,128]{3,2,1,0:T(8,128)(2,1)S(1)} %collective-permute-done.2.refs_3_), channel_id=1, source_target_pairs={{4,0},{8,4},{12,8},{16,12},{20,16},{24,20},{28,24},{5,1},{9,5},{13... | collective-permute-start | bytes 393224 | tf_op jit(solution)/shard_map/ppermute | solution.py:273
  25.3 5.8 %collective-permute-start.8 = (bf16[16,1,32,128]{3,2,1,0:T(8,128)(2,1)}, bf16[16,1,32,128]{3,2,1,0:T(8,128)(2,1)}, u32[]{:S(2)}, u32[]{:S(2)}) collective-permute-start(bf16[16,1,32,128]{3,2,1,0:T(8,128)(2,1)} %collective-permute-done.3.refs_4_), channel_id=1, source_target_pairs={{4,0},{8,4},{12,8},{16,12},{20,16},{24,20},{28,24},{5,1},{9,5},{13... | collective-permute-start | bytes 393224 | tf_op jit(solution)/shard_map/ppermute | solution.py:273
  26.6 1.2 %copy-start.2 = (bf16[16,2,64,256]{3,2,1,0:T(8,128)(2,1)S(1)}, bf16[16,2,64,256]{3,2,1,0:T(8,128)(2,1)}, u32[]{:S(2)}) copy-start(bf16[16,2,64,256]{3,2,1,0:T(8,128)(2,1)} %v_ref.1) | copy-start | bytes 3145732
  31.1 1.0 %copy-start.3 = (bf16[32,1,32,128]{3,2,1,0:T(8,128)(2,1)S(1)}, bf16[32,1,32,128]{3,2,1,0:T(8,128)(2,1)}, u32[]{:S(2)}) copy-start(bf16[32,1,32,128]{3,2,1,0:T(8,128)(2,1)} %refs_0_.1) | copy-start | bytes 786436
  41.3 15.7 %all-to-all-start = ((f32[8,16,432]{2,1,0:T(8,128)}), f32[8,16,432]{2,1,0:T(8,128)S(1)}, u32[]{:S(2)}, u32[]{:S(2)}) async-start(f32[8,16,432]{2,1,0:T(8,128)} %bitcast.1), calls=%async_computation | async-start | bytes 524288 | tf_op jit(solution)/shard_map/all_to_all | solution.py:295
  50.1 2.2 %copy-start.1 = (bf16[512,4096]{1,0:T(8,128)(2,1)S(1)}, bf16[512,4096]{1,0:T(8,128)(2,1)}, u32[]{:S(2)}) copy-start(bf16[512,4096]{1,0:T(8,128)(2,1)} %get-tuple-element.4.stack_ref) | copy-start | bytes 12582916

commit v2 on v0

--- a/solution.py
+++ b/solution.py
@@ -3,7 +3,152 @@
 import jax
 import jax.numpy as jnp
 from jax import lax
+from jax.experimental import pallas as pl
+from jax.experimental.pallas import tpu as pltpu
 from jax.sharding import PartitionSpec as P
+
+F32 = jnp.float32
+BF16 = jnp.bfloat16
+VMEM = pl.BlockSpec(memory_space=pltpu.VMEM)
+SMEM = pl.BlockSpec(memory_space=pltpu.SMEM)
+LIMIT = 48 * 1024 * 1024
+
+
+def ring_order(count):
+    return [0] + list(range(1, count, 2)) + list(range(2, count, 2))[::-1]
+
+
+def matmul(left, right):
+    return jnp.dot(left, right, preferred_element_type=F32)
+
+
+def one_hot(rows, cols, source):
+    row = lax.broadcasted_iota(jnp.int32, (rows, cols), 0)
+    col = lax.broadcasted_iota(jnp.int32, (rows, cols), 1)
+    return jnp.where(source(row, col), 1.0, 0.0).astype(BF16)
+
+
+def views_kernel(seats, behind_ref, volume_ref, weight_ref, views_ref, taps_ref, lines_ref):
+    chans, _, rows, cols = volume_ref.shape
+    channels = weight_ref.shape[2]
+    half = cols // 2
+    split = one_hot(cols, 3 * half, lambda row, col: row == 2 * (col & (half - 1)) + col // half - 1)
+    planes = [behind_ref.at[:, 0], volume_ref.at[:, 0], volume_ref.at[:, 1]]
+    for a, plane in enumerate(planes):
+        parted = matmul(plane[...].reshape(chans * rows, cols), split)
+        for e in range(3):
+            lines_ref[e] = parted[:, e * half : (e + 1) * half]
+        for row in range(rows):
+            places = [(1, row // 2)] if row % 2 == 0 else [(2, row // 2), (0, row // 2 + 1)]
+            for e in range(3):
+                line = lines_ref[e, pl.ds(row, chans, stride=rows), :].astype(BF16)
+                for b, r in places:
+                    if r < rows // 2:
+                        lo = (9 * a + 3 * b + e) * chans
+                        views_ref[lo : lo + chans, r * half : (r + 1) * half] = line
+        base = 9 * a * chans
+        views_ref[base : base + 3 * chans, :half] = jnp.zeros((3 * chans, half), BF16)
+    here = lax.axis_index("chan")
+    part = channels // len(seats)
+    row = lax.broadcasted_iota(jnp.int32, (channels, channels), 0)
+    col = lax.broadcasted_iota(jnp.int32, (channels, channels), 1)
+    order = jnp.zeros((channels, channels), jnp.bool_)
+    for slot in range(len(seats)):
+        owner = jnp.int32(0)
+        for chip in range(len(seats)):
+            owner = jnp.where(here == chip, seats[chip][slot], owner)
+        inside = (col >= slot * part) & (col < (slot + 1) * part)
+        order = order | (inside & (row == col + (owner - slot) * part))
+    order = jnp.where(order, 1.0, 0.0).astype(BF16)
+    ordered = matmul(weight_ref[...].reshape(27 * chans, channels), order).astype(BF16)
+    zero = jnp.zeros((chans, channels), BF16)
+    for k, e in enumerate((1, 2, 0)):
+        for b in range(3):
+            pick = lambda a: ordered[(9 * a + 3 * b + e) * chans : (9 * a + 3 * b + e + 1) * chans]
+            for plane, line in enumerate(((zero, pick(1)), (pick(0), pick(2)))):
+                lo = ((3 * plane + k) * 3 + b) * chans
+                taps_ref[lo : lo + chans, :] = jnp.concatenate(line, axis=1)
+
+
+def lines_kernel(*refs):
+    *parts, out_ref, wide_ref = refs
+    at = 0
+    for part in parts:
+        outs, _, rows, cols = part.shape
+        wide_ref[...] = part[...].reshape(outs * rows, cols).astype(F32)
+        for row in range(rows):
+            line = wide_ref[pl.ds(row, outs, stride=rows), :].astype(BF16)
+            out_ref[at : at + outs, row * cols : (row + 1) * cols] = line
+        at += outs
+
+
+def weight_kernel(seats, chans, *refs):
+    views_ref, *part_refs, out_ref, terms_ref, placed_ref = refs
+    channels = out_ref.shape[0]
+    grads = jnp.concatenate([ref[...] for ref in part_refs], axis=0)
+    terms_ref[: 27 * chans, :] = lax.dot_general(
+        views_ref[...], grads, (((1,), (1,)), ((), ())), preferred_element_type=F32
+    )
+    terms_ref[27 * chans :, :] = jnp.zeros((5 * chans, channels), F32)
+    for c in range(chans):
+        placed_ref[32 * c : 32 * c + 32, :] = terms_ref[pl.ds(c, 32, stride=chans), :]
+    turned = placed_ref[...].T
+    here = lax.axis_index("chan")
+    part = channels // len(seats)
+    for slot in range(len(seats)):
+        owner = jnp.int32(0)
+        for chip in range(len(seats)):
+            owner = jnp.where(here == chip, seats[chip][slot], owner)
+        place = pl.multiple_of(owner * part, part)
+        out_ref[pl.ds(place, part), :] = turned[slot * part : (slot + 1) * part]
+
+
+def input_kernel(parts, *refs):
+    taps_ref, *grad_refs, out_ref, cells_ref, lines_ref = refs
+    chans, _, rows, cols = out_ref.shape
+    half = cols // 2
+    grid_cells = half * rows // 2
+    grads = jnp.concatenate([ref[...] for ref in grad_refs], axis=0)
+    cells_ref[:, :grid_cells] = matmul(taps_ref[...], grads)
+    cells_ref[:, grid_cells:] = jnp.zeros((cells_ref.shape[0], half), F32)
+    group = 256 // chans
+    weave = one_hot(cols, cols, lambda row, col: col == 2 * (row & (half - 1)) + row // half)
+    inner = lax.broadcasted_iota(jnp.int32, (chans, half), 1) < half - 1
+
+    def cells(plane, kind, b, r):
+        lo = ((3 * plane + kind) * 3 + b) * chans
+        return cells_ref[lo : lo + chans, r * half : (r + 1) * half]
+
+    for plane in range(2):
+        for start in range(0, rows, group):
+            pieces = []
+            for row in range(start, start + group):
+                r = row // 2
+                if row % 2 == 0:
+                    even, odd, next_odd = [cells(plane, kind, 1, r) for kind in range(3)]
+                else:
+                    even, odd, next_odd = [
+                        cells(plane, kind, 0, r + 1) + cells(plane, kind, 2, r) for kind in range(3)
+                    ]
+                odd = odd + jnp.where(inner, pltpu.roll(next_odd, half - 1, 1), 0.0)
+                pieces.append(jnp.concatenate([even, odd], axis=1).astype(BF16))
+            woven = matmul(jnp.concatenate(pieces, axis=0), weave)
+            for side in range(2):
+                lanes = slice(side * half, (side + 1) * half)
+                lines_ref[side] = woven[:, lanes]
+                for c in range(chans):
+                    line = lines_ref[side, pl.ds(c, group, stride=chans), :].astype(BF16)
+                    out_ref[c, plane, start : start + group, lanes] = line
+
+
+def total_kernel(scale, terms_ref, out_ref):
+    chans, outs, taps = out_ref.shape
+    total = terms_ref[0]
+    for source in range(1, terms_ref.shape[0]):
+        total = total + terms_ref[source]
+    total = total * scale
+    for c in range(chans):
+        out_ref[c] = total[:, 32 * c : 32 * c + taps]
 
 
 def from_behind(shard, axis, by):
@@ -65,7 +210,7 @@
     )
 
 
-def shards(grad_out, volume, weight):
+def plain_shards(grad_out, volume, weight):
     plane_next = from_behind(grad_out, "depth", -1)
     grads_ext = jnp.concatenate([grad_out, plane_next], axis=1)
     channels_out = weight.shape[2]
@@ -80,7 +225,128 @@
     return (input_grad, summed * (1.0 / math.sqrt(cell_count)))
 
 
+def call(kernel, out_shape, *args, specs=None, scratch=(), cost=None):
+    flops, moved = cost
+    return pl.pallas_call(
+        kernel,
+        out_shape=out_shape,
+        in_specs=specs or [VMEM] * len(args),
+        out_specs=jax.tree.map(lambda _: VMEM, out_shape),
+        scratch_shapes=scratch,
+        compiler_params=pltpu.CompilerParams(vmem_limit_bytes=LIMIT),
+        cost_estimate=pl.CostEstimate(flops=flops, bytes_accessed=moved, transcendentals=0),
+    )(*args)
+
+
+def shards(grad_out, volume, weight):
+    count = lax.axis_size("chan")
+    depth = lax.axis_size("depth")
+    own_outs, _, rows, cols = grad_out.shape
+    chans = volume.shape[0]
+    channels = weight.shape[2]
+    cells = rows * cols
+    order = ring_order(count)
+    ahead = [(order[i], order[(i + 1) % count]) for i in range(count)]
+    back = [(b, a) for a, b in ahead]
+    farther = [(i, i + 1) for i in range(depth - 1)]
+    nearer = [(i, i - 1) for i in range(1, depth)]
+    shifts = [0]
+
+    near = []
+    up = down = grad_out
+    for step in range(1, (count - 1) // 2 + 1):
+        up = lax.ppermute(up, "chan", ahead)
+        down = lax.ppermute(down, "chan", back)
+        near += [up, down]
+        shifts += [-step, step]
+    last = lax.ppermute(up, "chan", ahead)
+    shifts += [count // 2]
+    seats = [[order[(order.index(chip) + s) % count] for s in shifts] for chip in range(count)]
+
+    next_own = lax.ppermute(grad_out, "depth", nearer)
+    behind = lax.ppermute(volume[:, 1:], "depth", farther)
+
+    own_weight = lax.dynamic_slice_in_dim(weight, lax.axis_index("chan") * chans, chans, 1)
+    views, taps = call(
+        lambda *refs: views_kernel(seats, *refs),
+        (
+            jax.ShapeDtypeStruct((27 * chans, cells), BF16),
+            jax.ShapeDtypeStruct((18 * chans, 2 * channels), BF16),
+        ),
+        behind,
+        volume,
+        own_weight,
+        scratch=(pltpu.VMEM((3, chans * 2 * rows, cols), F32),),
+        cost=(2 * 3 * 2 * cells * chans * 6 * cols, 6 << 20),
+    )
+
+    def lines(*parts):
+        return call(
+            lines_kernel,
+            jax.ShapeDtypeStruct((own_outs * len(parts), cells), BF16),
+            *parts,
+            scratch=(pltpu.VMEM((own_outs * rows, cols), F32),),
+            cost=(1 << 20, (len(parts) * own_outs * cells) << 2),
+        )
+
+    *near, views = lax.optimization_barrier((*near, views))
+    near_lines = lines(*near)
+    own_lines = lines(grad_out)
+    next_own_lines = lines(next_own)
+    next_near_lines = lax.ppermute(near_lines, "depth", nearer)
+    last_lines = lines(last)
+    next_last_lines = lax.ppermute(last_lines, "depth", nearer)
+    partial = call(
+        lambda *refs: weight_kernel(seats, chans, *refs),
+        jax.ShapeDtypeStruct((channels, 32 * chans), F32),
+        views,
+        own_lines,
+        near_lines,
+        last_lines,
+        scratch=(pltpu.VMEM((32 * chans, channels), F32), pltpu.VMEM((32 * chans, channels), F32)),
+        cost=(2 * 27 * chans * channels * cells, 8 << 20),
+    )
+    terms = lax.all_to_all(partial, "depth", split_axis=0, concat_axis=0, tiled=True)
+    input_grad = call(
+        lambda *refs: input_kernel(count, *refs),
+        jax.ShapeDtypeStruct(volume.shape, BF16),
+        taps,
+        next_own_lines,
+        next_near_lines,
+        next_last_lines,
+        own_lines,
+        near_lines,
+        last_lines,
+        scratch=(
+            pltpu.VMEM((18 * chans, cells + cols), F32),
+            pltpu.VMEM((2, 256, cols), F32),
+        ),
+        cost=(2 * 18 * chans * 2 * channels * cells, 8 << 20),
+    )
+    scale = 1.0 / math.sqrt(depth * cells)
+    outs = channels // depth
+    weight_grad = call(
+        lambda *refs: total_kernel(scale, *refs),
+        jax.ShapeDtypeStruct((chans, outs, 27), F32),
+        terms.reshape(depth, outs, 32 * chans),
+        cost=(1 << 20, 1 << 20),
+    )
+    return input_grad, jnp.transpose(weight_grad, (2, 0, 1))
+
+
 def solution(mesh):
     in_specs = (P("chan", "depth", None, None), P("chan", "depth", None, None), P())
     out_specs = (P("chan", "depth", None, None), P(None, "chan", "depth"))
-    return jax.shard_map(shards, mesh=mesh, in_specs=in_specs, out_specs=out_specs, check_vma=False)
+    ring = mesh.shape["chan"]
+
+    def either(grad_out, volume, weight):
+        fits = (
+            grad_out.shape[0] % 16 == 0
+            and volume.shape[0] == 16
+            and grad_out.shape[1] == 1
+            and ring % 2 == 0
+            and ring >= 4
+        )
+        return (shards if fits else plain_shards)(grad_out, volume, weight)
+
+    return jax.shard_map(either, mesh=mesh, in_specs=in_specs, out_specs=out_specs, check_vma=False)

time: 338 us -> 53.3 us (0.16)
  local copies, waits for them, and re-layouts: 153 us -> 2.41 us
  matrix products: 85.6 us -> 0 us
  other arithmetic: 39.4 us -> 0 us
  waiting for transfers between devices: 40.7 us -> 14.8 us
  starting transfers between devices: 1.5 us -> 23 us
  between operations: 14.1 us -> 0.74 us
  Pallas kernels: 0 us -> 12 us
    transpose x1 -> x0, matrix products: 83.6 us -> none  [weight_terms(): jnp.transpose(weight_cube, (2, 3, 4, 0, 1))]
    another operation x4 -> x0, local copies, waits for them, and re-layouts: 51.8 us -> none  [upsample(): paired = jnp.stack([even_cells, odd_cells], axis=coord_axis + 1)]
    another operation x6 -> x0, other arithmetic: 35.9 us -> none  [the longest x5 32 us: upsample(): paired = jnp.stack([even_cells, odd_cells], axis=coord_axis + 1)]
    slice x5 -> x1, local copies, waits for them, and re-layouts: 35.6 us -> 1.15 us  [shards(): behind = lax.ppermute(volume[:, 1:], 'depth', farther)]
    transpose x1 -> x0, local copies, waits for them, and re-layouts: 29.5 us -> none  [phase_grads(): along_h = upsample(jnp.moveaxis(along_w, 1, 0), 4, False)]
    all_gather x1 -> x0, waiting for transfers between devices: 29.3 us -> none  [shards(): every_channel = lax.all_gather(grads_ext, 'chan', axis=0, tiled=True)]
    broadcast_in_dim x2 -> x0, local copies, waits for them, and re-layouts: 28.1 us -> none  [the longest x1 23.1 us: weight_terms(): inputs[None]]
    pallas_call x0 -> x8, Pallas kernels: none -> 12 us  [call(): pl.pallas_call(kernel, out_shape=out_shape, in_specs=specs or [VMEM] * le...]
  transfers between devices with their start and end apart: 3 -> 8, of which waited for: 3 -> 3; matrix products, arithmetic and copies ran while one was open for 15% -> 0% of each run, Pallas kernels for 0% -> 17%
where the time goes in v2:
time: 53.3 us; the launch traced here: 53 us
  starting transfers between devices  23 us (43%)
  waiting for transfers between devices  14.8 us (28%)
  Pallas kernels  12 us (23%)
  local copies, waits for them, and re-layouts  2.41 us (5%)
  between operations  0.74 us (1%)
    pallas_call x8, Pallas kernels, call(): pl.pallas_call(kernel, out_shape=out_shape, in_specs=specs or [VMEM] * le...  12 us
    all_to_all x1, starting transfers between devices, shards(): lax.all_to_all(partial, 'depth', split_axis=0, concat_axis=0, tiled=True)  11 us
    all_to_all x1, waiting for transfers between devices, shards(): lax.all_to_all(partial, 'depth', split_axis=0, concat_axis=0, tiled=True)  6.58 us
    ppermute x1, waiting for transfers between devices, shards(): up = lax.ppermute(up, 'chan', ahead)  6.27 us
    ppermute x1, starting transfers between devices, shards(): up = lax.ppermute(up, 'chan', ahead)  2.46 us
    ppermute x1, starting transfers between devices, shards(): behind = lax.ppermute(volume[:, 1:], 'depth', farther)  2.39 us
    ppermute x1, starting transfers between devices, shards(): last = lax.ppermute(up, 'chan', ahead)  2.14 us
    ppermute x1, waiting for transfers between devices, shards(): last = lax.ppermute(up, 'chan', ahead)  1.96 us
  transfers between devices with their start and end apart: 8, of which 3 were waited for; matrix products, arithmetic and copies ran while one was open for 0% of the time, Pallas kernels for 17%

profile of v2, /device:TPU:0, one launch (start us, length us, event | category | flops | bytes accessed | tf_op | source)
XLA Modules:
  0.0 53.0 jit_solution(8781005997066297657)
XLA Ops:
  0.6 0.0 copy-start
  0.6 0.0 copy-start.2
  0.7 1.2 %slice.3 = bf16[16,1,64,256]{3,2,1,0:T(8,128)(2,1)S(1)} slice(bf16[16,2,64,256]{3,2,1,0:T(8,128)(2,1)} %refs_1_.1), slice={[0:16], [1:2], [0:64], [0:256]} | slice | bytes 1048576 | tf_op jit(solution)/shard_map/slice | solution.py:267
  1.8 2.4 %collective-permute-start = (bf16[16,1,64,256]{3,2,1,0:T(8,128)(2,1)S(1)}, bf16[16,1,64,256]{3,2,1,0:T(8,128)(2,1)S(1)}, u32[]{:S(2)}, u32[]{:S(2)}) collective-permute-start(bf16[16,1,64,256]{3,2,1,0:T(8,128)(2,1)S(1)} %slice.3), channel_id=1, source_target_pairs={{0,4},{4,8},{8,12},{12,16},{16,20},{20,24},{24,28},{1,5},{5,9},{9,... | collective-permute-start | bytes 1572872 | tf_op jit(solution)/shard_map/ppermute | solution.py:267
  4.2 2.5 %collective-permute-start.2 = (bf16[32,1,32,128]{3,2,1,0:T(8,128)(2,1)}, bf16[32,1,32,128]{3,2,1,0:T(8,128)(2,1)S(1)}, u32[]{:S(2)}, u32[]{:S(2)}) collective-permute-start(bf16[32,1,32,128]{3,2,1,0:T(8,128)(2,1)} %refs_0_.1), channel_id=1, source_target_pairs={{0,1},{1,3},{3,2},{2,0},{4,5},{5,7},{7,6},{6,4},{8,9},{9,11},{11,1... | collective-permute-start | bytes 786440 | tf_op jit(solution)/shard_map/ppermute | solution.py:258
  6.7 1.1 %collective-permute-start.3 = (bf16[32,1,32,128]{3,2,1,0:T(8,128)(2,1)}, bf16[32,1,32,128]{3,2,1,0:T(8,128)(2,1)S(1)}, u32[]{:S(2)}, u32[]{:S(2)}) collective-permute-start(bf16[32,1,32,128]{3,2,1,0:T(8,128)(2,1)} %refs_0_.1), channel_id=1, source_target_pairs={{1,0},{3,1},{2,3},{0,2},{5,4},{7,5},{6,7},{4,6},{9,8},{11,9},{10,1... | collective-permute-start | bytes 786440 | tf_op jit(solution)/shard_map/ppermute | solution.py:259
  7.8 0.0 copy-done
  7.8 6.3 %collective-permute-done.2.refs_0_ = bf16[32,1,32,128]{3,2,1,0:T(8,128)(2,1)S(1)} collective-permute-done((bf16[32,1,32,128]{3,2,1,0:T(8,128)(2,1)}, bf16[32,1,32,128]{3,2,1,0:T(8,128)(2,1)S(1)}, u32[]{:S(2)}, u32[]{:S(2)}) %collective-permute-start.2) | collective-permute-done | bytes 262176 | tf_op jit(solution)/shard_map/ppermute | solution.py:258
  14.0 2.1 %collective-permute-start.5 = (bf16[32,1,32,128]{3,2,1,0:T(8,128)(2,1)S(1)}, bf16[32,1,32,128]{3,2,1,0:T(8,128)(2,1)S(1)}, u32[]{:S(2)}, u32[]{:S(2)}) collective-permute-start(bf16[32,1,32,128]{3,2,1,0:T(8,128)(2,1)S(1)} %collective-permute-done.2.refs_0_), channel_id=1, source_target_pairs={{0,1},{1,3},{3,2},{2,0},{4,5},{5,7},{7,6},{6,4},{8,9},{9,11},{11,1... | collective-permute-start | bytes 786440 | tf_op jit(solution)/shard_map/ppermute | solution.py:262
  16.2 0.0 collective-permute-done.refs_0_
  16.2 0.0 copy-start.1
  16.2 1.2 %copy-done.1 = bf16[16,2,64,256]{3,2,1,0:T(8,128)(2,1)S(1)} copy-done((bf16[16,2,64,256]{3,2,1,0:T(8,128)(2,1)S(1)}, bf16[16,2,64,256]{3,2,1,0:T(8,128)(2,1)}, u32[]{:S(2)}) %copy-start.1) | copy-done | bytes 1048600
  17.4 4.7 %shard_map.50 = (bf16[432,4096]{1,0:T(8,128)(2,1)S(1)}, bf16[288,256]{1,0:T(8,128)(2,1)S(1)}) custom-call(bf16[16,1,64,256]{3,2,1,0:T(8,128)(2,1)S(1)} %collective-permute-done.refs_0_, bf16[16,2,64,256]{3,2,1,0:T(8,128)(2,1)S(1)} %copy-done.1, bf16[27,16,128]{2,1,0:T(8,128)(2,1)S(1)} %constant_dynamic-slice_fusion.refs_2_), custom_call_target="tpu_custom_call" | custom-call | flops 603979776 | bytes 6291456 | tf_op jit(solution)/shard_map/pallas_call | solution.py:230
  22.1 0.0 collective-permute-done.3.refs_1_
  22.1 0.7 %shard_map.52.refs_5_.refs_2_ = bf16[64,4096]{1,0:T(8,128)(2,1)S(1)} custom-call(bf16[32,1,32,128]{3,2,1,0:T(8,128)(2,1)S(1)} %collective-permute-done.2.refs_0_, bf16[32,1,32,128]{3,2,1,0:T(8,128)(2,1)S(1)} %collective-permute-done.3.refs_1_), custom_call_target="tpu_custom_call" | custom-call | flops 1048576 | bytes 1048576 | tf_op jit(solution)/shard_map/pallas_call | solution.py:230
  22.8 1.3 %collective-permute-start.4 = (bf16[64,4096]{1,0:T(8,128)(2,1)S(1)}, bf16[64,4096]{1,0:T(8,128)(2,1)S(1)}, u32[]{:S(2)}, u32[]{:S(2)}) collective-permute-start(bf16[64,4096]{1,0:T(8,128)(2,1)S(1)} %shard_map.52.refs_5_.refs_2_), channel_id=1, source_target_pairs={{4,0},{8,4},{12,8},{16,12},{20,16},{24,20},{28,24},{5,1},{9,5},{13... | collective-permute-start | bytes 1572872 | tf_op jit(solution)/shard_map/ppermute | solution.py:296
  24.1 0.0 copy-done.2
  24.1 1.3 %collective-permute-start.1 = (bf16[32,1,32,128]{3,2,1,0:T(8,128)(2,1)S(1)}, bf16[32,1,32,128]{3,2,1,0:T(8,128)(2,1)S(1)}, u32[]{:S(2)}, u32[]{:S(2)}) collective-permute-start(bf16[32,1,32,128]{3,2,1,0:T(8,128)(2,1)S(1)} %copy-done.2), channel_id=1, source_target_pairs={{4,0},{8,4},{12,8},{16,12},{20,16},{24,20},{28,24},{5,1},{9,5},{13... | collective-permute-start | bytes 786440 | tf_op jit(solution)/shard_map/ppermute | solution.py:266
  25.4 0.3 shard_map.54.refs_4_.refs_1_
  25.8 2.0 %collective-permute-done.5.refs_0_ = bf16[32,1,32,128]{3,2,1,0:T(8,128)(2,1)S(1)} collective-permute-done((bf16[32,1,32,128]{3,2,1,0:T(8,128)(2,1)S(1)}, bf16[32,1,32,128]{3,2,1,0:T(8,128)(2,1)S(1)}, u32[]{:S(2)}, u32[]{:S(2)}) %collective-permute-start.5) | collective-permute-done | bytes 262176 | tf_op jit(solution)/shard_map/ppermute | solution.py:262
  27.7 0.3 shard_map.53.refs_6_.refs_3_
  28.1 1.3 %collective-permute-start.6 = (bf16[32,4096]{1,0:T(8,128)(2,1)S(1)}, bf16[32,4096]{1,0:T(8,128)(2,1)S(1)}, u32[]{:S(2)}, u32[]{:S(2)}) collective-permute-start(bf16[32,4096]{1,0:T(8,128)(2,1)S(1)} %shard_map.53.refs_6_.refs_3_), channel_id=1, source_target_pairs={{4,0},{8,4},{12,8},{16,12},{20,16},{24,20},{28,24},{5,1},{9,5},{13... | collective-permute-start | bytes 786440 | tf_op jit(solution)/shard_map/ppermute | solution.py:298
  29.4 1.9 %shard_map.56 = f32[128,512]{1,0:T(8,128)} custom-call(bf16[432,4096]{1,0:T(8,128)(2,1)S(1)} %get-tuple-element.11.refs_0_, bf16[32,4096]{1,0:T(8,128)(2,1)S(1)} %shard_map.54.refs_4_.refs_1_, bf16[64,4096]{1,0:T(8,128)(2,1)S(1)} %shard_map.52.refs_5_.refs_2_, bf16[32,4096]{1,0:T(8,128)(2,1)S(1)} %shard_map.53.refs_6_.refs_3_), custom_call_target="tpu_custom_call" | custom-call | flops 452984832 | bytes 8388608 | tf_op jit(solution)/shard_map/pallas_call | solution.py:230
  31.3 11.0 %all-to-all-start = ((f32[8,16,512]{2,1,0:T(8,128)}), f32[8,16,512]{2,1,0:T(8,128)S(1)}, u32[]{:S(2)}, u32[]{:S(2)}) async-start(f32[8,16,512]{2,1,0:T(8,128)} %bitcast), calls=%async_computation | async-start | bytes 524288 | tf_op jit(solution)/shard_map/all_to_all | solution.py:309
  42.4 0.0 collective-permute-done.1.refs_0_
  42.4 0.3 shard_map.51.refs_1_
  42.7 6.6 %all-to-all-done.refs_0_ = f32[8,16,512]{2,1,0:T(8,128)S(1)} async-done(((f32[8,16,512]{2,1,0:T(8,128)}), f32[8,16,512]{2,1,0:T(8,128)S(1)}, u32[]{:S(2)}, u32[]{:S(2)}) %all-to-all-start) | async-done | bytes 262176 | tf_op jit(solution)/shard_map/all_to_all | solution.py:309
  49.3 0.8 %shard_map.57 = f32[16,16,27]{2,1,0:T(8,128)} custom-call(f32[8,16,512]{2,1,0:T(8,128)S(1)} %all-to-all-done.refs_0_), custom_call_target="tpu_custom_call" | custom-call | flops 1048576 | bytes 1048576 | tf_op jit(solution)/shard_map/pallas_call | solution.py:230
  50.1 0.0 collective-permute-done.6.refs_3_
  50.1 0.0 collective-permute-done.4.refs_2_
  50.1 2.9 %shard_map.55 = bf16[16,2,64,256]{3,2,1,0:T(8,128)(2,1)} custom-call(bf16[288,256]{1,0:T(8,128)(2,1)S(1)} %get-tuple-element.7.refs_0_, bf16[32,4096]{1,0:T(8,128)(2,1)S(1)} %shard_map.51.refs_1_, bf16[64,4096]{1,0:T(8,128)(2,1)S(1)} %collective-permute-done.4.refs_2_, bf16[32,4096]{1,0:T(8,128)(2,1)S(1)} %collective-permute-done.6.refs_3_, ...), custom_call_target="tpu_custom_call" | custom-call | flops 603979776 | bytes 8388608 | tf_op jit(solution)/shard_map/pallas_call | solution.py:230
  (1 shorter events, 0.0 us)
Async XLA Ops:
  0.6 7.1 %copy-start = (bf16[27,64,128]{2,1,0:T(8,128)(2,1)S(1)}, bf16[27,64,128]{2,1,0:T(8,128)(2,1)}, u32[]{:S(2)}) copy-start(bf16[27,64,128]{2,1,0:T(8,128)(2,1)} %param.5) | copy-start | bytes 1327108
  0.6 23.5 %copy-start.2 = (bf16[32,1,32,128]{3,2,1,0:T(8,128)(2,1)S(1)}, bf16[32,1,32,128]{3,2,1,0:T(8,128)(2,1)}, u32[]{:S(2)}) copy-start(bf16[32,1,32,128]{3,2,1,0:T(8,128)(2,1)} %refs_0_.1) | copy-start | bytes 786436
  1.8 14.4 %collective-permute-start = (bf16[16,1,64,256]{3,2,1,0:T(8,128)(2,1)S(1)}, bf16[16,1,64,256]{3,2,1,0:T(8,128)(2,1)S(1)}, u32[]{:S(2)}, u32[]{:S(2)}) collective-permute-start(bf16[16,1,64,256]{3,2,1,0:T(8,128)(2,1)S(1)} %slice.3), channel_id=1, source_target_pairs={{0,4},{4,8},{8,12},{12,16},{16,20},{20,24},{24,28},{1,5},{5,9},{9,... | collective-permute-start | bytes 1572872 | tf_op jit(solution)/shard_map/ppermute | solution.py:267
  4.2 9.8 %collective-permute-start.2 = (bf16[32,1,32,128]{3,2,1,0:T(8,128)(2,1)}, bf16[32,1,32,128]{3,2,1,0:T(8,128)(2,1)S(1)}, u32[]{:S(2)}, u32[]{:S(2)}) collective-permute-start(bf16[32,1,32,128]{3,2,1,0:T(8,128)(2,1)} %refs_0_.1), channel_id=1, source_target_pairs={{0,1},{1,3},{3,2},{2,0},{4,5},{5,7},{7,6},{6,4},{8,9},{9,11},{11,1... | collective-permute-start | bytes 786440 | tf_op jit(solution)/shard_map/ppermute | solution.py:258
  6.7 15.4 %collective-permute-start.3 = (bf16[32,1,32,128]{3,2,1,0:T(8,128)(2,1)}, bf16[32,1,32,128]{3,2,1,0:T(8,128)(2,1)S(1)}, u32[]{:S(2)}, u32[]{:S(2)}) collective-permute-start(bf16[32,1,32,128]{3,2,1,0:T(8,128)(2,1)} %refs_0_.1), channel_id=1, source_target_pairs={{1,0},{3,1},{2,3},{0,2},{5,4},{7,5},{6,7},{4,6},{9,8},{11,9},{10,1... | collective-permute-start | bytes 786440 | tf_op jit(solution)/shard_map/ppermute | solution.py:259
  14.0 13.7 %collective-permute-start.5 = (bf16[32,1,32,128]{3,2,1,0:T(8,128)(2,1)S(1)}, bf16[32,1,32,128]{3,2,1,0:T(8,128)(2,1)S(1)}, u32[]{:S(2)}, u32[]{:S(2)}) collective-permute-start(bf16[32,1,32,128]{3,2,1,0:T(8,128)(2,1)S(1)} %collective-permute-done.2.refs_0_), channel_id=1, source_target_pairs={{0,1},{1,3},{3,2},{2,0},{4,5},{5,7},{7,6},{6,4},{8,9},{9,11},{11,1... | collective-permute-start | bytes 786440 | tf_op jit(solution)/shard_map/ppermute | solution.py:262
  16.2 1.2 %copy-start.1 = (bf16[16,2,64,256]{3,2,1,0:T(8,128)(2,1)S(1)}, bf16[16,2,64,256]{3,2,1,0:T(8,128)(2,1)}, u32[]{:S(2)}) copy-start(bf16[16,2,64,256]{3,2,1,0:T(8,128)(2,1)} %refs_1_.1) | copy-start | bytes 3145732
  22.8 27.3 %collective-permute-start.4 = (bf16[64,4096]{1,0:T(8,128)(2,1)S(1)}, bf16[64,4096]{1,0:T(8,128)(2,1)S(1)}, u32[]{:S(2)}, u32[]{:S(2)}) collective-permute-start(bf16[64,4096]{1,0:T(8,128)(2,1)S(1)} %shard_map.52.refs_5_.refs_2_), channel_id=1, source_target_pairs={{4,0},{8,4},{12,8},{16,12},{20,16},{24,20},{28,24},{5,1},{9,5},{13... | collective-permute-start | bytes 1572872 | tf_op jit(solution)/shard_map/ppermute | solution.py:296
  24.1 18.2 %collective-permute-start.1 = (bf16[32,1,32,128]{3,2,1,0:T(8,128)(2,1)S(1)}, bf16[32,1,32,128]{3,2,1,0:T(8,128)(2,1)S(1)}, u32[]{:S(2)}, u32[]{:S(2)}) collective-permute-start(bf16[32,1,32,128]{3,2,1,0:T(8,128)(2,1)S(1)} %copy-done.2), channel_id=1, source_target_pairs={{4,0},{8,4},{12,8},{16,12},{20,16},{24,20},{28,24},{5,1},{9,5},{13... | collective-permute-start | bytes 786440 | tf_op jit(solution)/shard_map/ppermute | solution.py:266
  28.1 22.0 %collective-permute-start.6 = (bf16[32,4096]{1,0:T(8,128)(2,1)S(1)}, bf16[32,4096]{1,0:T(8,128)(2,1)S(1)}, u32[]{:S(2)}, u32[]{:S(2)}) collective-permute-start(bf16[32,4096]{1,0:T(8,128)(2,1)S(1)} %shard_map.53.refs_6_.refs_3_), channel_id=1, source_target_pairs={{4,0},{8,4},{12,8},{16,12},{20,16},{24,20},{28,24},{5,1},{9,5},{13... | collective-permute-start | bytes 786440 | tf_op jit(solution)/shard_map/ppermute | solution.py:298
  31.3 18.0 %all-to-all-start = ((f32[8,16,512]{2,1,0:T(8,128)}), f32[8,16,512]{2,1,0:T(8,128)S(1)}, u32[]{:S(2)}, u32[]{:S(2)}) async-start(f32[8,16,512]{2,1,0:T(8,128)} %bitcast), calls=%async_computation | async-start | bytes 524288 | tf_op jit(solution)/shard_map/all_to_all | solution.py:309
